TPU v7x, 32 devices: a whole 2x2x4 slice. The times are simulated.
32 devices in a mesh: group: 2 (over y), req: 4 (over z), tensor: 4 (over x, core).
Axes of the slice: x: 2, y: 2, z: 4, core: 2. Of those that a mesh axis runs over, the one named last changes fastest.
Arguments:
- hidden: bfloat16 [256, 28672], P(('group', 'req')), parts along dimension 0, may hold values from -6 to 6
- down_weight: bfloat16 [28672, 8192], P('req', 'tensor'), may hold values from -0.03125 to 0.03125
- adapter_input_weight: bfloat16 [8, 64, 28672], P('req', None, 'tensor'), may hold values from -0.03125 to 0.03125
- adapter_output_weight: bfloat16 [8, 64, 8192], P('req', None, 'tensor'), may hold values from -0.75 to 0.75
- adapter_storage_index: int32 [16], P('group'), parts along dimension 0, may hold values from 0 to 7, as said below
- row_adapter_index: int32 [256], P(('group', 'req')), parts along dimension 0, may hold values from 0 to 7, as said below
Outputs:
- mixed: bfloat16 [256, 8192], P(('group', 'req'), 'tensor'), parts along dimension 0
There are 2 independent parts, one for each index of `group`. A program takes and returns all parts, laid end to end along the dimension named above; an argument that names none is the same for every part. Nothing has to cross between parts.
Inputs may be any that keep to these rules, and one draw needn't show every extreme that they name: `adapter_storage_index`: each adapter has its own storage index. `row_adapter_index`: among the 32 rows of one index of req, at most 24 name adapters whose storage index // 2 is the same; in every draw, each index of req has exactly 24 rows for some one owner, which need not be the same owner for different indices.
All inputs are finite; a program needn't handle non-finite values.
Results may differ from a plain program's by a relative error of at most 0.005.
Values may be sent and summed in bfloat16 or wider, within the bound.
A program may use at most 128 MiB of HBM per device.

v0:
```python
import jax
import jax.numpy as jnp
from jax import lax
from jax.sharding import PartitionSpec as P


def per_device(
    hidden,
    down_weight,
    adapter_input_weight,
    adapter_output_weight,
    adapter_storage_index,
    row_adapter_index,
):
    req_count = lax.axis_size("req")
    tensor_pos = lax.axis_index("tensor")
    row_count = hidden.shape[0]
    hidden_slice = adapter_input_weight.shape[2]
    resident_adapters = adapter_input_weight.shape[0]
    capacity = min(row_count, 3 * ((row_count + req_count - 1) // req_count))
    slot_count = req_count * capacity
    spread = lax.all_to_all(hidden, "req", split_axis=1, concat_axis=0, tiled=True)
    lookup_table_index = jnp.arange(adapter_storage_index.shape[0], dtype=jnp.int32)
    storage = jnp.sum(
        jnp.where(
            row_adapter_index[:, None] == lookup_table_index[None, :],
            adapter_storage_index[None, :],
            0,
        ),
        axis=1,
    )
    owner = storage // resident_adapters
    within = storage % resident_adapters
    row_index = jnp.arange(row_count, dtype=jnp.int32)
    before = jnp.sum(
        (owner[:, None] == owner[None, :]) & (row_index[:, None] > row_index[None, :]), axis=1
    )
    target = owner * capacity + before
    placed = jnp.arange(slot_count, dtype=jnp.int32)[:, None] == target[None, :]
    feature_part = lax.dynamic_slice_in_dim(hidden, tensor_pos * hidden_slice, hidden_slice, 1)
    send_rows = jnp.dot(
        placed.astype(jnp.bfloat16), feature_part, preferred_element_type=jnp.float32
    ).astype(jnp.bfloat16)
    send_adapter = jnp.sum(jnp.where(placed, within[None, :] + 1, 0), axis=1) - 1
    send_source = jnp.sum(jnp.where(placed, row_index[None, :], 0), axis=1)
    received_rows, got_adapter, got_source = (
        lax.all_to_all(
            send_rows.reshape(req_count, capacity, hidden_slice),
            "req",
            split_axis=0,
            concat_axis=0,
            tiled=True,
        ),
        lax.all_to_all(
            send_adapter.reshape(req_count, capacity),
            "req",
            split_axis=0,
            concat_axis=0,
            tiled=True,
        ),
        lax.all_to_all(
            send_source.reshape(req_count, capacity), "req", split_axis=0, concat_axis=0, tiled=True
        ),
    )
    received_rows = received_rows.reshape(slot_count, hidden_slice)
    got_adapter = got_adapter.reshape(slot_count)
    got_source = got_source.reshape(slot_count)
    low_rank_inner = jnp.einsum(
        "qd,ind->qin", received_rows, adapter_input_weight, preferred_element_type=jnp.float32
    )
    chosen = got_adapter[:, None] == jnp.arange(resident_adapters, dtype=jnp.int32)[None, :]
    low_rank_inner = jnp.where(chosen[:, :, None], low_rank_inner, jnp.float32(0.0))
    low_rank_inner = lax.psum(low_rank_inner, "tensor").astype(jnp.bfloat16)
    adapter_delta = jnp.einsum(
        "bcm,cmx->bx", low_rank_inner, adapter_output_weight, preferred_element_type=jnp.float32
    ).astype(jnp.bfloat16)
    reduced = lax.psum_scatter(
        jnp.dot(spread, down_weight, preferred_element_type=jnp.float32),
        "req",
        scatter_dimension=0,
        tiled=True,
    )
    returned = lax.all_to_all(
        adapter_delta.reshape(req_count, capacity, adapter_delta.shape[1]),
        "req",
        split_axis=0,
        concat_axis=0,
        tiled=True,
    )
    returned = returned.reshape(slot_count, adapter_delta.shape[1])
    reduced = reduced + jnp.dot(
        placed.T.astype(jnp.bfloat16), returned, preferred_element_type=jnp.float32
    )
    return reduced.astype(jnp.bfloat16)


def solution(mesh):
    in_specs = (
        P(("group", "req"), None),
        P("req", "tensor"),
        P("req", None, "tensor"),
        P("req", None, "tensor"),
        P("group"),
        P(("group", "req")),
    )
    out_specs = P(("group", "req"), "tensor")
    return jax.shard_map(
        per_device, mesh=mesh, in_specs=in_specs, out_specs=out_specs, check_vma=False
    )
```

profile of v0, /device:TPU:0, one launch (start us, length us, event | category | flops | bytes accessed | tf_op | source)
XLA Modules:
  0.0 154.4 jit_solution(2739853783332171323)
XLA Ops:
  6.5 0.0 copy-start
  6.5 0.9 select_reduce_fusion.1
  7.4 0.2 convert_reduce_fusion
  7.6 0.1 select_reduce_fusion
  7.7 0.7 sub.14
  8.4 6.3 %all-to-all-start.1 = ((s32[4,1,24]{2,1,0:T(1,128)}), s32[4,1,24]{2,1,0:T(1,128)S(1)}, u32[]{:S(2)}, u32[]{:S(2)}) async-start(s32[4,1,24]{2,1,0:T(1,128)} %bitcast.2), calls=%async_computation.2 | async-start | bytes 4096 | tf_op jit(solution)/shard_map/all_to_all | solution.py:54
  14.7 2.8 %copy.14 = bf16[4,4,8,7168]{3,2,0,1:T(8,128)(2,1)} copy(bf16[4,4,8,7168]{3,2,1,0:T(8,128)(2,1)} %bitcast.27) | data formatting | bytes 3670016 | tf_op jit(solution)/shard_map/all_to_all | solution.py:22
  17.6 2.6 %all-to-all-done.1 = s32[4,1,24]{2,1,0:T(1,128)S(1)} async-done(((s32[4,1,24]{2,1,0:T(1,128)}), s32[4,1,24]{2,1,0:T(1,128)S(1)}, u32[]{:S(2)}, u32[]{:S(2)}) %all-to-all-start.1) | async-done | bytes 416 | tf_op jit(solution)/shard_map/all_to_all | solution.py:54
  20.2 4.4 %all-to-all-start = ((bf16[32,4,7168]{2,0,1:T(8,128)(2,1)}), bf16[32,4,7168]{2,0,1:T(8,128)(2,1)}, u32[]{:S(2)}, u32[]{:S(2)}) async-start(bf16[32,4,7168]{2,0,1:T(8,128)(2,1)} %bitcast.25), calls=%async_computation | async-start | bytes 3670016 | tf_op jit(solution)/shard_map/all_to_all | solution.py:22
  24.6 2.7 %convolution_convert_fusion = bf16[96,7168]{1,0:T(8,128)(2,1)} fusion(bf16[32,28672]{1,0:T(8,128)(2,1)} %param.6, s32[]{:T(128)S(6)} %select_n.46, s32[32]{0:T(128)S(1)} %multiply_add_fusion), kind=kOutput, calls=%fused_computation | convolution fusion | flops 44731392 | bytes 1835140 | tf_op jit(solution)/shard_map/dot_general | solution.py:41
  27.3 38.7 %all-to-all-done = bf16[32,4,7168]{2,0,1:T(8,128)(2,1)} async-done(((bf16[32,4,7168]{2,0,1:T(8,128)(2,1)}), bf16[32,4,7168]{2,0,1:T(8,128)(2,1)}, u32[]{:S(2)}, u32[]{:S(2)}) %all-to-all-start) | async-done | bytes 1835040 | tf_op jit(solution)/shard_map/all_to_all | solution.py:22
  66.1 3.5 %all-to-all-start.2 = ((bf16[4,24,7168]{2,1,0:T(8,128)(2,1)}), bf16[4,24,7168]{2,1,0:T(8,128)(2,1)S(1)}, u32[]{:S(2)}, u32[]{:S(2)}) async-start(bf16[4,24,7168]{2,1,0:T(8,128)(2,1)} %bitcast.3), calls=%async_computation.3 | async-start | bytes 2752512 | tf_op jit(solution)/shard_map/all_to_all | solution.py:47
  69.6 0.0 reduce-scatter.2.cloned.1.call-start
  69.7 14.9 %fusion.9 = f32[128,2048]{1,0:T(8,128)} fusion(bf16[128,7168]{1,0:T(8,128)(2,1)} %bitcast.1, bf16[7168,2048]{1,0:T(8,128)(2,1)} %param.7), kind=kOutput, calls=%fused_computation.28 | convolution fusion | flops 3758096384 | bytes 32243712 | tf_op jit(solution)/shard_map/dot_general | solution.py:78
  84.5 0.0 reduce-scatter.2.cloned.1.call-update
  84.6 0.5 broadcast.158
  85.1 0.7 reduce.3
  85.7 0.1 eq.69
  85.8 31.7 %all-to-all-done.2 = bf16[4,24,7168]{2,1,0:T(8,128)(2,1)S(1)} async-done(((bf16[4,24,7168]{2,1,0:T(8,128)(2,1)}), bf16[4,24,7168]{2,1,0:T(8,128)(2,1)S(1)}, u32[]{:S(2)}, u32[]{:S(2)}) %all-to-all-start.2) | async-done | bytes 1376288 | tf_op jit(solution)/shard_map/all_to_all | solution.py:47
  117.5 0.0 copy-done
  117.5 0.6 convolution_select_fusion
  118.2 10.7 %psum.7 = bf16[96,2,64]{0,2,1:T(8,128)(2,1)S(1)} all-reduce(f32[96,2,64]{0,2,1:T(8,128)S(1)} %convolution_select_fusion), channel_id=1, replica_groups=mesh['group'=2,'req'=4,'tensor'=4] {'tensor'}, use_global_device_ids=true, to_apply=%region_4.5 | all-reduce | flops 12288 | bytes 73728 | tf_op jit(solution)/shard_map/psum | solution.py:73
  128.8 1.3 fusion
  130.2 15.5 %all_to_all.35 = bf16[4,24,2048]{2,1,0:T(8,128)(2,1)S(1)} all-to-all(bf16[4,24,2048]{2,1,0:T(8,128)(2,1)S(1)} %bitcast.29), channel_id=1, replica_groups=mesh['group'=2,'req'=4,'tensor'=4] {'req'}, dimensions={0} | all-to-all | bytes 786432 | tf_op jit(solution)/shard_map/all_to_all | solution.py:83
  145.7 0.0 reduce-scatter.2.cloned.1.call-done
  145.7 1.9 %fusion.1 = bf16[32,2048]{1,0:T(8,128)(2,1)} fusion(f32[32,2048]{1,0:T(8,128)} %reduce-scatter.2.cloned.1.call-done, bf16[96,2048]{1,0:T(8,128)(2,1)S(1)} %bitcast.28, s32[32]{0:T(128)S(1)} %multiply_add_fusion), kind=kOutput, calls=%fused_computation.4 | convolution fusion | flops 12717056 | bytes 786560 | tf_op jit(solution)/shard_map/dot_general | solution.py:91
  (4 shorter events, 0.0 us)
Async XLA Ops:
  6.5 111.0 %copy-start = (bf16[2,64,7168]{2,1,0:T(8,128)(2,1)S(1)}, bf16[2,64,7168]{2,1,0:T(8,128)(2,1)}, u32[]{:S(2)}) copy-start(bf16[2,64,7168]{2,1,0:T(8,128)(2,1)} %param.8) | copy-start | bytes 5505028
  8.4 11.8 %all-to-all-start.1 = ((s32[4,1,24]{2,1,0:T(1,128)}), s32[4,1,24]{2,1,0:T(1,128)S(1)}, u32[]{:S(2)}, u32[]{:S(2)}) async-start(s32[4,1,24]{2,1,0:T(1,128)} %bitcast.2), calls=%async_computation.2 | async-start | bytes 4096 | tf_op jit(solution)/shard_map/all_to_all | solution.py:54
  20.2 45.9 %all-to-all-start = ((bf16[32,4,7168]{2,0,1:T(8,128)(2,1)}), bf16[32,4,7168]{2,0,1:T(8,128)(2,1)}, u32[]{:S(2)}, u32[]{:S(2)}) async-start(bf16[32,4,7168]{2,0,1:T(8,128)(2,1)} %bitcast.25), calls=%async_computation | async-start | bytes 3670016 | tf_op jit(solution)/shard_map/all_to_all | solution.py:22
  66.1 51.4 %all-to-all-start.2 = ((bf16[4,24,7168]{2,1,0:T(8,128)(2,1)}), bf16[4,24,7168]{2,1,0:T(8,128)(2,1)S(1)}, u32[]{:S(2)}, u32[]{:S(2)}) async-start(bf16[4,24,7168]{2,1,0:T(8,128)(2,1)} %bitcast.3), calls=%async_computation.3 | async-start | bytes 2752512 | tf_op jit(solution)/shard_map/all_to_all | solution.py:47
  69.6 76.1 %reduce-scatter.2.cloned.1.call-start = ((), (), s32[]{:S(2)}) async-start(), calls=%async_computation.5 | async-start | bytes 1310720 | tf_op jit(solution)/shard_map/reduce_scatter | solution.py:77
Sparse Core Ops, SparseCore 0:
  84.7 33.6 reduce-scatter.1
where the time goes:
time: 155 us; the launch traced here: 154 us
  waiting for transfers between devices  73.1 us (47%)
  blocking collectives  26.2 us (17%)
  matrix products  21.4 us (14%)
  starting transfers between devices  14.3 us (9%)
  between operations  13.5 us (9%)
  local copies, waits for them, and re-layouts  4.11 us (3%)
  other arithmetic  1.86 us (1%)
    all_to_all x1, waiting for transfers between devices, per_device(): lax.all_to_all(hidden, 'req', split_axis=1, concat_axis=0, tiled=True)  38.7 us
    all_to_all x1, waiting for transfers between devices, per_device(): lax.all_to_all(send_rows.reshape(req_count, capacity, hidden_slice), 'req...  31.7 us
    all_to_all x1, blocking collectives, per_device(): lax.all_to_all(adapter_delta.reshape(req_count, capacity, adapter_delta.s...  15.5 us
    dot_general x1, matrix products, per_device(): jnp.dot(spread, down_weight, preferred_element_type=jnp.float32)  14.9 us
    psum x1, blocking collectives, per_device(): low_rank_inner = lax.psum(low_rank_inner, 'tensor').astype(jnp.bfloat16)  10.7 us
    all_to_all x1, starting transfers between devices, per_device(): lax.all_to_all(send_adapter.reshape(req_count, capacity), 'req', split_ax...  6.32 us
    all_to_all x1, starting transfers between devices, per_device(): lax.all_to_all(hidden, 'req', split_axis=1, concat_axis=0, tiled=True)  4.39 us
    all_to_all x1, starting transfers between devices, per_device(): lax.all_to_all(send_rows.reshape(req_count, capacity, hidden_slice), 'req...  3.54 us
  transfers between devices with their start and end apart: 4, of which 3 were waited for; matrix products, arithmetic and copies ran while one was open for 15% of the time, Pallas kernels for 0%

commit v1 on v0

v1 whole, which is shorter than its diff:
```python
import functools

import jax
import jax.numpy as jnp
from jax import lax
from jax.experimental import pallas as pl
from jax.experimental.pallas import tpu as pltpu
from jax.sharding import PartitionSpec as P

MESH = pl.DeviceIdType.MESH


def tile_of(extent, most):
    size = min(extent, most)
    while extent % size:
        size //= 2
    return size


def kernel(
    n_r,
    n_t,
    piece,
    rank,
    table_ref,
    row_ref,
    hidden_ref,
    w_ref,
    a_ref,
    b_ref,
    out_ref,
    gathered,
    base_in,
    w_v,
    a_v,
    b_v,
    acc,
    store_all,
    inner,
    inner_slots,
    part_send,
    part_slots,
    own_sem,
    ownb_sem,
    w_sem,
    ab_sem,
    g_send,
    g_recv,
    h_send,
    h_recv,
    st_send,
    st_recv,
    in_send,
    in_recv,
    p_send,
    p_recv,
):
    q = lax.axis_index("req")
    t = lax.axis_index("tensor")
    rows, units = hidden_ref.shape
    lanes, width = b_ref.shape
    resident = lanes // rank
    base_units, adapter_units = units // n_r, units // n_t
    c_base, c_adapter = base_units // piece, adapter_units // piece
    home = (q * base_units) // adapter_units
    first = (q * base_units) % adapter_units // piece if c_base != c_adapter else 0
    my_rows = pl.ds(pl.multiple_of(q * rows, rows), rows)

    def block(b):
        return pl.ds(pl.multiple_of(b * rows, rows), rows)

    def own_slice(c):
        return hidden_ref.at[:, pl.ds(pl.multiple_of(t * adapter_units + c * piece, 128), piece)]

    own = [
        pltpu.make_async_copy(own_slice(c), gathered.at[c, my_rows, :], own_sem.at[c])
        for c in range(c_adapter)
    ]
    own_base = [
        pltpu.make_async_copy(
            hidden_ref.at[:, pl.ds(pl.multiple_of(q * base_units + j * piece, 128), piece)],
            base_in.at[j, my_rows, :],
            ownb_sem.at[j],
        )
        for j in range(c_base)
    ]
    load_w = [
        pltpu.make_async_copy(
            w_ref.at[pl.ds(j * piece, piece), :], w_v.at[pl.ds(j * piece, piece), :], w_sem.at[j]
        )
        for j in range(c_base)
    ]
    load_a = pltpu.make_async_copy(a_ref, a_v, ab_sem.at[0])
    load_b = pltpu.make_async_copy(b_ref, b_v, ab_sem.at[1])

    barrier = pltpu.get_barrier_semaphore()

    @pl.loop(1, n_r)
    def _(i):
        pl.semaphore_signal(
            barrier, inc=1, device_id={"req": lax.rem(q + i, n_r)}, device_id_type=MESH
        )

    @pl.loop(1, n_t)
    def _(i):
        pl.semaphore_signal(
            barrier, inc=1, device_id={"tensor": lax.rem(t + i, n_t)}, device_id_type=MESH
        )

    own[0].start()
    own_base[0].start()
    load_a.start()
    for c in range(1, c_adapter):
        own[c].start()
    for j in range(c_base):
        if j:
            own_base[j].start()
        load_w[j].start()
    load_b.start()

    row_at = lax.broadcasted_iota(jnp.int32, (rows, lanes), 0)

    def put_row(r, held):
        return jnp.where(row_at == r, table_ref[row_ref[r]], held)

    store_all[my_rows, :] = lax.fori_loop(0, rows, put_row, jnp.zeros((rows, lanes), jnp.int32))
    acc[...] = jnp.zeros_like(acc)
    inner[...] = jnp.zeros_like(inner)
    pl.semaphore_wait(barrier, n_r + n_t - 2)

    def pass_on(b, c, to, side, from_own):
        return pltpu.make_async_remote_copy(
            src_ref=own_slice(c) if from_own else gathered.at[c, block(b), :],
            dst_ref=gathered.at[c, block(b), :],
            send_sem=g_send.at[side, b, c],
            recv_sem=g_recv.at[b, c],
            device_id={"req": to},
            device_id_type=MESH,
        )

    def send_own(c):
        @pl.when(q < n_r - 1)
        def _():
            pass_on(q, c, q + 1, 0, True).start()

        @pl.when(q > 0)
        def _():
            pass_on(q, c, q - 1, 1, True).start()

    def to_mate(b, c, j, i):
        return pltpu.make_async_remote_copy(
            src_ref=gathered.at[c, block(b), :],
            dst_ref=base_in.at[j, block(b), :],
            send_sem=h_send.at[i - 1, b, j],
            recv_sem=h_recv.at[b, j],
            device_id={"tensor": lax.rem(t + i, n_t)},
            device_id_type=MESH,
        )

    def to_self(b, c, j):
        return pltpu.make_async_copy(
            gathered.at[c, block(b), :], base_in.at[j, block(b), :], h_recv.at[b, j]
        )

    def store_copy(i):
        return pltpu.make_async_remote_copy(
            src_ref=store_all.at[my_rows, :],
            dst_ref=store_all.at[my_rows, :],
            send_sem=st_send.at[i],
            recv_sem=st_recv.at[q],
            device_id={"req": lax.rem(q + i, n_r)},
            device_id_type=MESH,
        )

    send_own(0)

    @pl.loop(1, n_r)
    def _(i):
        store_copy(i).start()

    send_own(1)

    row_tile = tile_of(n_r * rows, 128)
    col_tile = tile_of(width, 512)

    for c in range(c_adapter):
        in_base = (c >= first) & (c < first + c_base)
        j = c - first

        def arrived(b, forward, side):
            pass_on(b, c, 0, side, False).wait_recv()

            @pl.when((forward >= 0) & (forward < n_r))
            def _():
                pass_on(b, c, forward, side, False).start()

            @pl.when((t == home) & in_base)
            def _():
                for i in range(1, n_t):
                    to_mate(b, c, j, i).start()
                to_self(b, c, j).start()

        @pl.loop(1, n_r)
        def _(k):
            @pl.when(q - k >= 0)
            def _():
                arrived(q - k, q + 1, 0)

            @pl.when(q + k < n_r)
            def _():
                arrived(q + k, q - 1, 1)

        if c + 2 < c_adapter:
            send_own(c + 2)
        if c == 0:
            load_a.wait()
        own[c].wait()

        @pl.loop(0, n_r * rows // row_tile)
        def _(m):
            at = pl.ds(pl.multiple_of(m * row_tile, row_tile), row_tile)
            inner[at, :] += lax.dot_general(
                gathered[c, at, :],
                a_v[:, pl.ds(c * piece, piece)],
                (((1,), (1,)), ((), ())),
                preferred_element_type=jnp.float32,
            )

        @pl.when(in_base)
        def _():
            pltpu.make_async_copy(
                hidden_ref.at[:, pl.ds(0, piece)], base_in.at[j, my_rows, :], ownb_sem.at[j]
            ).wait()
            pltpu.make_async_copy(
                w_ref.at[pl.ds(0, piece), :], w_v.at[pl.ds(0, piece), :], w_sem.at[j]
            ).wait()

            @pl.loop(1, n_r)
            def _(i):
                to_self(lax.rem(q + i, n_r), c, j).wait()

            @pl.loop(0, n_r * rows // row_tile)
            def _(m):
                at = pl.ds(pl.multiple_of(m * row_tile, row_tile), row_tile)

                @pl.loop(0, width // col_tile)
                def _(n):
                    cols = pl.ds(pl.multiple_of(n * col_tile, col_tile), col_tile)
                    acc[at, cols] += jnp.dot(
                        base_in[j, at, :],
                        w_v[pl.ds(pl.multiple_of(j * piece, piece), piece), cols],
                        preferred_element_type=jnp.float32,
                    )

    @pl.loop(1, n_r)
    def _(i):
        pltpu.make_async_copy(
            store_all.at[my_rows, :],
            store_all.at[block(lax.rem(q + i, n_r)), :],
            st_recv.at[lax.rem(q + i, n_r)],
        ).wait()

    lane_adapter = lax.broadcasted_iota(jnp.int32, (n_r * rows, lanes), 1) // rank + q * resident
    inner[...] = jnp.where(store_all[...] == lane_adapter, inner[...], jnp.float32(0.0))

    def inner_copy(i):
        return pltpu.make_async_remote_copy(
            src_ref=inner,
            dst_ref=inner_slots.at[t],
            send_sem=in_send.at[i],
            recv_sem=in_recv.at[t],
            device_id={"tensor": lax.rem(t + i, n_t)},
            device_id_type=MESH,
        )

    def inner_arrival(i):
        mate = lax.rem(t + i, n_t)
        return pltpu.make_async_copy(inner, inner_slots.at[mate], in_recv.at[mate])

    @pl.loop(1, n_t)
    def _(i):
        inner_copy(i).start()

    load_b.wait()

    @pl.loop(1, n_t)
    def _(i):
        inner_arrival(i).wait()

    inner_slots[t] = inner[...]
    total = inner_slots[0]
    for s in range(1, n_t):
        total = total + inner_slots[s]

    def part_copy(d, i):
        return pltpu.make_async_remote_copy(
            src_ref=part_send.at[d],
            dst_ref=part_slots.at[q],
            send_sem=p_send.at[i],
            recv_sem=p_recv.at[q],
            device_id={"req": d},
            device_id_type=MESH,
        )

    inner_slots[0] = total

    def finish_block(d):
        low = inner_slots[0, block(d), :].astype(jnp.bfloat16)
        delta = jnp.dot(low, b_v[...], preferred_element_type=jnp.float32).astype(jnp.bfloat16)
        return acc[block(d), :] + delta.astype(jnp.float32)

    @pl.loop(1, n_r)
    def _(i):
        d = lax.rem(q + i, n_r)
        part_send[d] = finish_block(d).astype(jnp.bfloat16)
        part_copy(d, i).start()

    acc[my_rows, :] = finish_block(q)

    @pl.loop(1, n_r)
    def _(i):
        s = lax.rem(q + i, n_r)
        pltpu.make_async_copy(part_send.at[s], part_slots.at[s], p_recv.at[s]).wait()
        acc[my_rows, :] += part_slots[s].astype(jnp.float32)

    out_ref[...] = acc[my_rows, :].astype(jnp.bfloat16)

    @pl.loop(1, n_r)
    def _(i):
        part_copy(lax.rem(q + i, n_r), i).wait_send()
        store_copy(i).wait_send()

    @pl.loop(1, n_t)
    def _(i):
        inner_copy(i).wait_send()

    for c in range(c_adapter):
        in_base = (c >= first) & (c < first + c_base)
        j = c - first

        @pl.loop(0, n_r)
        def _(b):
            @pl.when((b <= q) & (q < n_r - 1))
            def _():
                pass_on(b, c, 0, 0, False).wait_send()

            @pl.when((b >= q) & (q > 0))
            def _():
                pass_on(b, c, 0, 1, False).wait_send()

            @pl.when((b != q) & (t == home) & in_base)
            def _():
                for i in range(1, n_t):
                    to_mate(b, c, j, i).wait_send()


def per_device(
    n_r,
    n_t,
    hidden,
    down_weight,
    adapter_input_weight,
    adapter_output_weight,
    adapter_storage_index,
    row_adapter_index,
):
    rows, units = hidden.shape
    resident, rank, adapter_units = adapter_input_weight.shape
    base_units, width = down_weight.shape
    lanes = resident * rank
    piece = min(base_units, adapter_units // 4)
    c_base, c_adapter = base_units // piece, adapter_units // piece
    everyone = n_r * rows
    hbm = pl.BlockSpec(memory_space=pl.ANY)
    smem = pl.BlockSpec(memory_space=pltpu.SMEM)
    bf16, f32 = jnp.bfloat16, jnp.float32
    dma = pltpu.SemaphoreType.DMA
    return pl.pallas_call(
        functools.partial(kernel, n_r, n_t, piece, rank),
        out_shape=jax.ShapeDtypeStruct((rows, width), bf16),
        in_specs=[smem, smem, hbm, hbm, hbm, hbm],
        out_specs=pl.BlockSpec(memory_space=pltpu.VMEM),
        scratch_shapes=[
            pltpu.VMEM((c_adapter, everyone, piece), bf16),
            pltpu.VMEM((c_base, everyone, piece), bf16),
            pltpu.VMEM((base_units, width), bf16),
            pltpu.VMEM((lanes, adapter_units), bf16),
            pltpu.VMEM((lanes, width), bf16),
            pltpu.VMEM((everyone, width), f32),
            pltpu.VMEM((everyone, lanes), jnp.int32),
            pltpu.VMEM((everyone, lanes), f32),
            pltpu.VMEM((n_t, everyone, lanes), f32),
            pltpu.VMEM((n_r, rows, width), bf16),
            pltpu.VMEM((n_r, rows, width), bf16),
            dma((c_adapter,)),
            dma((c_base,)),
            dma((c_base,)),
            dma((2,)),
            dma((2, n_r, c_adapter)),
            dma((n_r, c_adapter)),
            dma((n_t - 1, n_r, c_base)),
            dma((n_r, c_base)),
            dma((n_r,)),
            dma((n_r,)),
            dma((n_t,)),
            dma((n_t,)),
            dma((n_r,)),
            dma((n_r,)),
        ],
        compiler_params=pltpu.CompilerParams(
            collective_id=0, has_side_effects=True, vmem_limit_bytes=56 * 1024 * 1024
        ),
    )(
        adapter_storage_index,
        row_adapter_index,
        hidden,
        down_weight,
        adapter_input_weight.reshape(lanes, adapter_units),
        adapter_output_weight.reshape(lanes, width),
    )


def solution(mesh):
    in_specs = (
        P(("group", "req"), None),
        P("req", "tensor"),
        P("req", None, "tensor"),
        P("req", None, "tensor"),
        P("group"),
        P(("group", "req")),
    )
    out_specs = P(("group", "req"), "tensor")
    return jax.shard_map(
        functools.partial(per_device, mesh.shape["req"], mesh.shape["tensor"]),
        mesh=mesh,
        in_specs=in_specs,
        out_specs=out_specs,
        check_vma=False,
    )
```

time: 155 us -> 74.9 us (0.48)
  Pallas kernels: 0 us -> 73.1 us
  waiting for transfers between devices: 73.1 us -> 0 us
  blocking collectives: 26.2 us -> 0 us
  matrix products: 21.4 us -> 0 us
  starting transfers between devices: 14.3 us -> 0 us
  between operations: 13.5 us -> 0.01 us
  local copies, waits for them, and re-layouts: 4.11 us -> 1.57 us
  other arithmetic: 1.86 us -> 0 us
    pallas_call x0 -> x1, Pallas kernels: none -> 73.1 us  [per_device(): pl.pallas_call(functools.partial(kernel, n_r, n_t, piece, rank), out_shap...]
    all_to_all x3 -> x0, waiting for transfers between devices: 73.1 us -> none  [the longest x1 38.7 us: per_device(): lax.all_to_all(hidden, 'req', split_axis=1, concat_axis=0, tiled=True)]
    dot_general x5 -> x0, matrix products: 21.4 us -> none  [the longest x1 14.9 us: per_device(): jnp.dot(spread, down_weight, preferred_element_type=jnp.float32)]
    all_to_all x1 -> x0, blocking collectives: 15.5 us -> none  [per_device(): lax.all_to_all(adapter_delta.reshape(req_count, capacity, adapter_delta.s...]
    all_to_all x3 -> x0, starting transfers between devices: 14.3 us -> none  [the longest x1 6.32 us: per_device(): lax.all_to_all(send_adapter.reshape(req_count, capacity), 'req', split_ax...]
    psum x1 -> x0, blocking collectives: 10.7 us -> none  [per_device(): low_rank_inner = lax.psum(low_rank_inner, 'tensor').astype(jnp.bfloat16)]
    all_to_all x2 -> x0, local copies, waits for them, and re-layouts: 3.36 us -> none  [the longest x1 2.84 us: per_device(): lax.all_to_all(hidden, 'req', split_axis=1, concat_axis=0, tiled=True)]
    unnamed x2 -> x1, local copies, waits for them, and re-layouts: 0.01 us -> 1.57 us
  transfers between devices with their start and end apart: 4 -> 0, of which waited for: 3 -> 0; matrix products, arithmetic and copies ran while one was open for 15% -> 0% of each run, Pallas kernels for 0% -> 0%
where the time goes in v1:
time: 74.9 us; the launch traced here: 74.7 us
  Pallas kernels  73.1 us (98%)
  local copies, waits for them, and re-layouts  1.57 us (2%)
    pallas_call x1, Pallas kernels, per_device(): pl.pallas_call(functools.partial(kernel, n_r, n_t, piece, rank), out_shap...  73.1 us
    unnamed x1, local copies, waits for them, and re-layouts  1.57 us

profile of v1, /device:TPU:0, one launch (start us, length us, event | category | flops | bytes accessed | tf_op | source)
XLA Modules:
  0.0 74.7 jit_solution(2945404968530856116)
XLA Ops:
  0.0 73.1 %shard_map.64 = bf16[32,2048]{1,0:T(8,128)(2,1)} custom-call(s32[8]{0:T(128)} %table_ref.1, s32[32]{0:T(128)} %row_ref.1, bf16[32,28672]{1,0:T(8,128)(2,1)} %hidden_ref.1, bf16[7168,2048]{1,0:T(8,128)(2,1)} %w_ref.1, bf16[128,7168]{1,0:T(8,128)(2,1)} %bitcast.2, bf16[128,2048]{1,0:T(8,128)(2,1)} %bitcast.3), custom_call_target="tpu_custom_call" | custom-call | tf_op jit(solution)/shard_map/pallas_call | solution.py:378
  73.1 1.6 %copy.8 = bf16[32,2048]{1,0:T(8,128)(2,1)} copy(bf16[32,2048]{1,0:T(8,128)(2,1)} %shard_map.64) | data formatting | bytes 262144

commit v2 on v1

--- a/solution.py
+++ b/solution.py
@@ -40,6 +40,9 @@
     inner_slots,
     part_send,
     part_slots,
+    a_help,
+    help_out,
+    help_in,
     own_sem,
     ownb_sem,
     w_sem,
@@ -54,6 +57,9 @@
     in_recv,
     p_send,
     p_recv,
+    ah_sem,
+    help_send,
+    help_recv,
 ):
     q = lax.axis_index("req")
     t = lax.axis_index("tensor")
@@ -125,8 +131,42 @@
 
     store_all[my_rows, :] = lax.fori_loop(0, rows, put_row, jnp.zeros((rows, lanes), jnp.int32))
     acc[...] = jnp.zeros_like(acc)
-    inner[...] = jnp.zeros_like(inner)
     pl.semaphore_wait(barrier, n_r + n_t - 2)
+
+    lent_from = c_adapter // 2 if n_r >= 4 else c_adapter
+    last_home = ((n_r - 1) * base_units) // adapter_units
+    lends_low = lax.rem(t, 2) == 1
+    lends_high = lax.rem(t + last_home, 2) == 1
+
+    def lent(to):
+        return ((to == 0) & lends_low) | ((to == n_r - 1) & lends_high)
+
+    def travels(c, to):
+        return jnp.logical_not(lent(to)) if c >= lent_from else to >= 0
+
+    lends = lent(q)
+    helps = ((q == 1) & lends_low) | ((q == n_r - 2) & lends_high)
+    lent_columns = pl.ds(lent_from * piece, (c_adapter - lent_from) * piece)
+
+    def lend_copy():
+        return pltpu.make_async_remote_copy(
+            src_ref=a_ref.at[:, lent_columns],
+            dst_ref=a_help,
+            send_sem=ah_sem.at[0],
+            recv_sem=ah_sem.at[1],
+            device_id={"req": jnp.where(q == 0, 1, n_r - 2)},
+            device_id_type=MESH,
+        )
+
+    def help_copy(b):
+        return pltpu.make_async_remote_copy(
+            src_ref=help_out.at[block(b), :],
+            dst_ref=help_in.at[block(b), :],
+            send_sem=help_send.at[b],
+            recv_sem=help_recv.at[b],
+            device_id={"req": jnp.where(q == 1, 0, n_r - 1)},
+            device_id_type=MESH,
+        )
 
     def pass_on(b, c, to, side, from_own):
         return pltpu.make_async_remote_copy(
@@ -139,21 +179,25 @@
         )
 
     def send_own(c):
-        @pl.when(q < n_r - 1)
+        @pl.when((q < n_r - 1) & travels(c, q + 1))
         def _():
             pass_on(q, c, q + 1, 0, True).start()
 
-        @pl.when(q > 0)
+        @pl.when((q > 0) & travels(c, q - 1))
         def _():
             pass_on(q, c, q - 1, 1, True).start()
 
-    def to_mate(b, c, j, i):
+    paired = t + 1 - 2 * lax.rem(t, 2)
+    relays = (lax.rem(t, 2) == lax.rem(home, 2)) & (t != home)
+
+    def to_mate(b, c, j, i, relayed):
+        to = paired if i == 0 else lax.rem(t + 2 * i, n_t)
         return pltpu.make_async_remote_copy(
-            src_ref=gathered.at[c, block(b), :],
+            src_ref=base_in.at[j, block(b), :] if relayed else gathered.at[c, block(b), :],
             dst_ref=base_in.at[j, block(b), :],
-            send_sem=h_send.at[i - 1, b, j],
+            send_sem=h_send.at[i, b, j],
             recv_sem=h_recv.at[b, j],
-            device_id={"tensor": lax.rem(t + i, n_t)},
+            device_id={"tensor": to},
             device_id_type=MESH,
         )
 
@@ -172,59 +216,114 @@
             device_id_type=MESH,
         )
 
-    send_own(0)
-
-    @pl.loop(1, n_r)
-    def _(i):
-        store_copy(i).start()
-
-    send_own(1)
-
-    row_tile = tile_of(n_r * rows, 128)
-    col_tile = tile_of(width, 512)
+    def inner_copy(b, i):
+        return pltpu.make_async_remote_copy(
+            src_ref=inner.at[block(b), :],
+            dst_ref=inner_slots.at[t, block(b), :],
+            send_sem=in_send.at[i, b],
+            recv_sem=in_recv.at[t, b],
+            device_id={"tensor": lax.rem(t + i, n_t)},
+            device_id_type=MESH,
+        )
+
+    def part_copy(d):
+        return pltpu.make_async_remote_copy(
+            src_ref=part_send.at[d],
+            dst_ref=part_slots.at[q],
+            send_sem=p_send.at[d],
+            recv_sem=p_recv.at[q],
+            device_id={"req": d},
+            device_id_type=MESH,
+        )
 
     for c in range(c_adapter):
-        in_base = (c >= first) & (c < first + c_base)
-        j = c - first
-
-        def arrived(b, forward, side):
+        send_own(c)
+        if c == 0:
+
+            @pl.loop(1, n_r)
+            def _(i):
+                store_copy(i).start()
+
+            if lent_from < c_adapter:
+
+                @pl.when(lends)
+                def _():
+                    lend_copy().start()
+
+    col_tile = tile_of(width, 1024)
+
+    def base_chunk(c):
+        return (c >= first) & (c < first + c_base), c - first
+
+    def arrive(b, c, forward, side):
+        in_base, j = base_chunk(c)
+
+        @pl.when(travels(c, q))
+        def _():
             pass_on(b, c, 0, side, False).wait_recv()
 
-            @pl.when((forward >= 0) & (forward < n_r))
-            def _():
-                pass_on(b, c, forward, side, False).start()
-
-            @pl.when((t == home) & in_base)
-            def _():
-                for i in range(1, n_t):
-                    to_mate(b, c, j, i).start()
-                to_self(b, c, j).start()
-
-        @pl.loop(1, n_r)
-        def _(k):
-            @pl.when(q - k >= 0)
-            def _():
-                arrived(q - k, q + 1, 0)
-
-            @pl.when(q + k < n_r)
-            def _():
-                arrived(q + k, q - 1, 1)
-
-        if c + 2 < c_adapter:
-            send_own(c + 2)
-        if c == 0:
-            load_a.wait()
-        own[c].wait()
-
-        @pl.loop(0, n_r * rows // row_tile)
-        def _(m):
-            at = pl.ds(pl.multiple_of(m * row_tile, row_tile), row_tile)
-            inner[at, :] += lax.dot_general(
+        @pl.when((forward >= 0) & (forward < n_r) & travels(c, forward))
+        def _():
+            pass_on(b, c, forward, side, False).start()
+
+        @pl.when((t == home) & in_base)
+        def _():
+            for i in reversed(range(n_t // 2)):
+                to_mate(b, c, j, i, False).start()
+            to_self(b, c, j).start()
+
+    def rank_product(b, c):
+        at = block(b)
+
+        @pl.when(travels(c, q) | (b == q))
+        def _():
+            product = lax.dot_general(
                 gathered[c, at, :],
                 a_v[:, pl.ds(c * piece, piece)],
                 (((1,), (1,)), ((), ())),
                 preferred_element_type=jnp.float32,
             )
+            if c == 0:
+                inner[at, :] = product
+            else:
+                inner[at, :] += product
+
+    def base_product(at, c):
+        in_base, j = base_chunk(c)
+
+        @pl.when(in_base)
+        def _():
+            @pl.loop(0, width // col_tile)
+            def _(n):
+                cols = pl.ds(pl.multiple_of(n * col_tile, col_tile), col_tile)
+                acc[at, cols] += jnp.dot(
+                    base_in[j, at, :],
+                    w_v[pl.ds(pl.multiple_of(j * piece, piece), piece), cols],
+                    preferred_element_type=jnp.float32,
+                )
+
+    def ready(b, c):
+        in_base, j = base_chunk(c)
+
+        @pl.when(in_base)
+        def _():
+            to_self(b, c, j).wait()
+
+            @pl.when(relays)
+            def _():
+                to_mate(b, c, j, 0, True).start()
+
+    def multiply(b, c):
+        ready(b, c)
+        rank_product(b, c)
+        base_product(block(b), c)
+
+    def multiply_near(c):
+        own[c].wait()
+        both(1, lambda b, to, side: ready(b, c))
+        rank_product(q, c)
+        both(1, lambda b, to, side: rank_product(b, c))
+        in_base, j = base_chunk(c)
 
         @pl.when(in_base)
         def _():
@@ -235,87 +334,134 @@
                 w_ref.at[pl.ds(0, piece), :], w_v.at[pl.ds(0, piece), :], w_sem.at[j]
             ).wait()
 
-            @pl.loop(1, n_r)
-            def _(i):
-                to_self(lax.rem(q + i, n_r), c, j).wait()
-
-            @pl.loop(0, n_r * rows // row_tile)
-            def _(m):
-                at = pl.ds(pl.multiple_of(m * row_tile, row_tile), row_tile)
-
-                @pl.loop(0, width // col_tile)
-                def _(n):
-                    cols = pl.ds(pl.multiple_of(n * col_tile, col_tile), col_tile)
-                    acc[at, cols] += jnp.dot(
-                        base_in[j, at, :],
-                        w_v[pl.ds(pl.multiple_of(j * piece, piece), piece), cols],
-                        preferred_element_type=jnp.float32,
-                    )
+        at_end = (q == 0) | (q == n_r - 1)
+        start = pl.multiple_of(jnp.maximum(q - 1, 0) * rows, rows)
+
+        @pl.when(at_end)
+        def _():
+            base_product(pl.ds(start, 2 * rows), c)
+
+        if n_r > 2:
+
+            @pl.when(jnp.logical_not(at_end))
+            def _():
+                base_product(pl.ds(start, 3 * rows), c)
+
+    def assist(b):
+        at = block(b)
+        help_out[at, :] = sum(
+            lax.dot_general(
+                gathered[c, at, :],
+                a_help[:, pl.ds((c - lent_from) * piece, piece)],
+                (((1,), (1,)), ((), ())),
+                preferred_element_type=jnp.float32,
+            )
+            for c in range(lent_from, c_adapter)
+        )
+        help_copy(b).start()
+
+    def assist_from(b, to, side):
+        @pl.when(helps & jnp.where(side == 0, q == n_r - 2, q == 1))
+        def _():
+            assist(b)
+
+    def exchange(b, mine):
+        at = block(b)
+        if not mine:
+            pltpu.make_async_copy(store_all.at[my_rows, :], store_all.at[at, :], st_recv.at[b]).wait()
+
+            @pl.when(lends)
+            def _():
+                pltpu.make_async_copy(
+                    help_out.at[at, :], help_in.at[at, :], help_recv.at[b]
+                ).wait()
+                inner[at, :] += help_in[at, :]
+
+        lane_adapter = lax.broadcasted_iota(jnp.int32, (rows, lanes), 1) // rank + q * resident
+        inner[at, :] = jnp.where(store_all[at, :] == lane_adapter, inner[at, :], jnp.float32(0.0))
+
+        @pl.loop(1, n_t)
+        def _(i):
+            inner_copy(b, i).start()
+
+    def finish(b):
+        at = block(b)
+
+        @pl.loop(1, n_t)
+        def _(i):
+            mate = lax.rem(t + i, n_t)
+            pltpu.make_async_copy(
+                inner.at[at, :], inner_slots.at[mate, at, :], in_recv.at[mate, b]
+            ).wait()
+
+        inner_slots[t, at, :] = inner[at, :]
+        total = inner_slots[0, at, :]
+        for s in range(1, n_t):
+            total = total + inner_slots[s, at, :]
+        delta = jnp.dot(
+            total.astype(jnp.bfloat16), b_v[...], preferred_element_type=jnp.float32
+        ).astype(jnp.bfloat16)
+        return acc[at, :] + delta.astype(jnp.float32)
+
+    def both(k, act):
+        @pl.when((q - k >= 0) & (k > 0))
+        def _():
+            act(q - k, q + 1, 0)
+
+        @pl.when((q + k < n_r) & (k > 0))
+        def _():
+            act(q + k, q - 1, 1)
+
+    def hand_back(b, *_):
+        part_send[b] = finish(b).astype(jnp.bfloat16)
+        part_copy(b).start()
+
+    last = c_adapter - 1
+    load_a.wait()
 
     @pl.loop(1, n_r)
-    def _(i):
-        pltpu.make_async_copy(
-            store_all.at[my_rows, :],
-            store_all.at[block(lax.rem(q + i, n_r)), :],
-            st_recv.at[lax.rem(q + i, n_r)],
-        ).wait()
-
-    lane_adapter = lax.broadcasted_iota(jnp.int32, (n_r * rows, lanes), 1) // rank + q * resident
-    inner[...] = jnp.where(store_all[...] == lane_adapter, inner[...], jnp.float32(0.0))
-
-    def inner_copy(i):
-        return pltpu.make_async_remote_copy(
-            src_ref=inner,
-            dst_ref=inner_slots.at[t],
-            send_sem=in_send.at[i],
-            recv_sem=in_recv.at[t],
-            device_id={"tensor": lax.rem(t + i, n_t)},
-            device_id_type=MESH,
-        )
-
-    def inner_arrival(i):
-        mate = lax.rem(t + i, n_t)
-        return pltpu.make_async_copy(inner, inner_slots.at[mate], in_recv.at[mate])
-
-    @pl.loop(1, n_t)
-    def _(i):
-        inner_copy(i).start()
-
-    load_b.wait()
-
-    @pl.loop(1, n_t)
-    def _(i):
-        inner_arrival(i).wait()
-
-    inner_slots[t] = inner[...]
-    total = inner_slots[0]
-    for s in range(1, n_t):
-        total = total + inner_slots[s]
-
-    def part_copy(d, i):
-        return pltpu.make_async_remote_copy(
-            src_ref=part_send.at[d],
-            dst_ref=part_slots.at[q],
-            send_sem=p_send.at[i],
-            recv_sem=p_recv.at[q],
-            device_id={"req": d},
-            device_id_type=MESH,
-        )
-
-    inner_slots[0] = total
-
-    def finish_block(d):
-        low = inner_slots[0, block(d), :].astype(jnp.bfloat16)
-        delta = jnp.dot(low, b_v[...], preferred_element_type=jnp.float32).astype(jnp.bfloat16)
-        return acc[block(d), :] + delta.astype(jnp.float32)
-
-    @pl.loop(1, n_r)
-    def _(i):
-        d = lax.rem(q + i, n_r)
-        part_send[d] = finish_block(d).astype(jnp.bfloat16)
-        part_copy(d, i).start()
-
-    acc[my_rows, :] = finish_block(q)
+    def _(k):
+        for c in range(c_adapter):
+            both(k, lambda b, to, side: arrive(b, c, to, side))
+
+            if c:
+
+                @pl.when(k == 1)
+                def _():
+                    multiply_near(c - 1)
+
+                @pl.when(k > 1)
+                def _():
+                    both(k, lambda b, to, side: multiply(b, c - 1))
+            else:
+
+                @pl.when(k == 2)
+                def _():
+                    multiply_near(last)
+                    exchange(q, True)
+                    load_b.wait()
+
+                @pl.when(k > 2)
+                def _():
+                    both(k - 1, lambda b, to, side: multiply(b, last))
+            if c == min(1, last) and lent_from < c_adapter:
+
+                @pl.when((k == 2) & helps)
+                def _():
+                    lend_copy().wait_recv()
+                    assist(q)
+
+                both(k - 1, assist_from)
+            if c == min(2, last):
+                both(k - 2, hand_back)
+            if c == last:
+                both(k - 1, lambda b, to, side: exchange(b, False))
+
+    both(n_r - 1, lambda b, to, side: multiply(b, last))
+    both(n_r - 1, lambda b, to, side: exchange(b, False))
+    both(n_r - 2, hand_back)
+    acc[my_rows, :] = finish(q)
+    both(n_r - 1, hand_back)
 
     @pl.loop(1, n_r)
     def _(i):
@@ -325,33 +471,48 @@
 
     out_ref[...] = acc[my_rows, :].astype(jnp.bfloat16)
 
+    if lent_from < c_adapter:
+
+        @pl.when(lends)
+        def _():
+            lend_copy().wait_send()
+
+        @pl.loop(0, n_r)
+        def _(b):
+            @pl.when(helps & jnp.where(q == 1, b > 0, b < n_r - 1))
+            def _():
+                help_copy(b).wait_send()
+
     @pl.loop(1, n_r)
     def _(i):
-        part_copy(lax.rem(q + i, n_r), i).wait_send()
+        part_copy(lax.rem(q + i, n_r)).wait_send()
         store_copy(i).wait_send()
 
-    @pl.loop(1, n_t)
-    def _(i):
-        inner_copy(i).wait_send()
-
-    for c in range(c_adapter):
-        in_base = (c >= first) & (c < first + c_base)
-        j = c - first
-
-        @pl.loop(0, n_r)
-        def _(b):
-            @pl.when((b <= q) & (q < n_r - 1))
+    @pl.loop(0, n_r)
+    def _(b):
+        @pl.loop(1, n_t)
+        def _(i):
+            inner_copy(b, i).wait_send()
+
+        for c in range(c_adapter):
+            in_base, j = base_chunk(c)
+
+            @pl.when((b <= q) & (q < n_r - 1) & travels(c, q + 1))
             def _():
                 pass_on(b, c, 0, 0, False).wait_send()
 
-            @pl.when((b >= q) & (q > 0))
+            @pl.when((b >= q) & (q > 0) & travels(c, q - 1))
             def _():
                 pass_on(b, c, 0, 1, False).wait_send()
 
             @pl.when((b != q) & (t == home) & in_base)
             def _():
-                for i in range(1, n_t):
-                    to_mate(b, c, j, i).wait_send()
+                for i in range(n_t // 2):
+                    to_mate(b, c, j, i, False).wait_send()
+
+            @pl.when((b != q) & relays & in_base)
+            def _():
+                to_mate(b, c, j, 0, True).wait_send()
 
 
 def per_device(
@@ -392,18 +553,24 @@
             pltpu.VMEM((n_t, everyone, lanes), f32),
             pltpu.VMEM((n_r, rows, width), bf16),
             pltpu.VMEM((n_r, rows, width), bf16),
+            pltpu.VMEM((lanes, piece * c_adapter // 2), bf16),
+            pltpu.VMEM((everyone, lanes), f32),
+            pltpu.VMEM((everyone, lanes), f32),
             dma((c_adapter,)),
             dma((c_base,)),
             dma((c_base,)),
             dma((2,)),
             dma((2, n_r, c_adapter)),
             dma((n_r, c_adapter)),
-            dma((n_t - 1, n_r, c_base)),
+            dma((n_t // 2, n_r, c_base)),
             dma((n_r, c_base)),
             dma((n_r,)),
             dma((n_r,)),
-            dma((n_t,)),
-            dma((n_t,)),
+            dma((n_t, n_r)),
+            dma((n_t, n_r)),
+            dma((n_r,)),
+            dma((n_r,)),
+            dma((2,)),
             dma((n_r,)),
             dma((n_r,)),
         ],

time: 74.9 us -> 66.5 us (0.89)
  Pallas kernels: 73.1 us -> 64.7 us
    pallas_call x1, Pallas kernels: 73.1 us -> 64.7 us  [per_device(): pl.pallas_call(functools.partial(kernel, n_r, n_t, piece, rank), out_shap...]
where the time goes in v2:
time: 66.5 us; the launch traced here: 66.3 us
  Pallas kernels  64.7 us (97%)
  local copies, waits for them, and re-layouts  1.57 us (2%)
    pallas_call x1, Pallas kernels, per_device(): pl.pallas_call(functools.partial(kernel, n_r, n_t, piece, rank), out_shap...  64.7 us
    unnamed x1, local copies, waits for them, and re-layouts  1.57 us

profile of v2, /device:TPU:0, one launch (start us, length us, event | category | flops | bytes accessed | tf_op | source)
XLA Modules:
  0.0 66.3 jit_solution(17906389677604233893)
XLA Ops:
  0.0 64.7 %shard_map.64 = bf16[32,2048]{1,0:T(8,128)(2,1)} custom-call(s32[8]{0:T(128)} %table_ref.1, s32[32]{0:T(128)} %row_ref.1, bf16[32,28672]{1,0:T(8,128)(2,1)} %hidden_ref.1, bf16[7168,2048]{1,0:T(8,128)(2,1)} %w_ref.1, bf16[128,7168]{1,0:T(8,128)(2,1)} %bitcast.2, bf16[128,2048]{1,0:T(8,128)(2,1)} %bitcast.3), custom_call_target="tpu_custom_call" | custom-call | tf_op jit(solution)/shard_map/pallas_call | solution.py:539
  64.7 1.6 %copy.8 = bf16[32,2048]{1,0:T(8,128)(2,1)} copy(bf16[32,2048]{1,0:T(8,128)(2,1)} %shard_map.64) | data formatting | bytes 262144

commit v3 on v2

--- a/solution.py
+++ b/solution.py
@@ -181,11 +181,11 @@
     def send_own(c):
         @pl.when((q < n_r - 1) & travels(c, q + 1))
         def _():
-            pass_on(q, c, q + 1, 0, True).start()
+            pass_on(q, c, q + 1, 0, False).start()
 
         @pl.when((q > 0) & travels(c, q - 1))
         def _():
-            pass_on(q, c, q - 1, 1, True).start()
+            pass_on(q, c, q - 1, 1, False).start()
 
     paired = t + 1 - 2 * lax.rem(t, 2)
     relays = (lax.rem(t, 2) == lax.rem(home, 2)) & (t != home)
@@ -237,6 +237,7 @@
         )
 
     for c in range(c_adapter):
+        own[c].wait()
         send_own(c)
         if c == 0:
 
@@ -319,7 +320,6 @@
         base_product(block(b), c)
 
     def multiply_near(c):
-        own[c].wait()
         both(1, lambda b, to, side: ready(b, c))
         rank_product(q, c)
         both(1, lambda b, to, side: rank_product(b, c))

time: 66.5 us -> 66.3 us (level)
  no operation moved by 1% of the time
where the time goes in v3:
time: 66.3 us; the launch traced here: 66.2 us
  Pallas kernels  64.6 us (97%)
  local copies, waits for them, and re-layouts  1.57 us (2%)
    pallas_call x1, Pallas kernels, per_device(): pl.pallas_call(functools.partial(kernel, n_r, n_t, piece, rank), out_shap...  64.6 us
    unnamed x1, local copies, waits for them, and re-layouts  1.57 us

profile of v3, /device:TPU:0, one launch (start us, length us, event | category | flops | bytes accessed | tf_op | source)
XLA Modules:
  0.0 66.2 jit_solution(13287274765593425170)
XLA Ops:
  0.0 64.6 %shard_map.64 = bf16[32,2048]{1,0:T(8,128)(2,1)} custom-call(s32[8]{0:T(128)} %table_ref.1, s32[32]{0:T(128)} %row_ref.1, bf16[32,28672]{1,0:T(8,128)(2,1)} %hidden_ref.1, bf16[7168,2048]{1,0:T(8,128)(2,1)} %w_ref.1, bf16[128,7168]{1,0:T(8,128)(2,1)} %bitcast.2, bf16[128,2048]{1,0:T(8,128)(2,1)} %bitcast.3), custom_call_target="tpu_custom_call" | custom-call | tf_op jit(solution)/shard_map/pallas_call | solution.py:539
  64.6 1.6 %copy.8 = bf16[32,2048]{1,0:T(8,128)(2,1)} copy(bf16[32,2048]{1,0:T(8,128)(2,1)} %shard_map.64) | data formatting | bytes 262144
